TPU v7x, 128 devices: a whole 4x4x4 slice. The times are simulated.
128 devices in a mesh: aa: 16 (over x_hi, z, core), ba: 8 (over y, x_lo).
Axes of the slice: x: 4 (x_hi: 2, x_lo: 2; x = x_hi * 2 + x_lo), y: 4, z: 4, core: 2. Of those that a mesh axis runs over, the one named last changes fastest.
Arguments:
- field: bfloat16 [1024, 1024, 1024], P(None, 'aa', 'ba'), may hold values from -8 to 8
- mode_one: bfloat16 [1024, 256], replicated, may hold values from -0.1875 to 0.1875
- mode_two: bfloat16 [1024, 256], P('aa'), may hold values from -0.1875 to 0.1875
Outputs:
- gram: float32 [1024, 1024], P('ba')
All inputs are finite; a program needn't handle non-finite values.
Results may differ from a plain program's by a relative error of at most 0.00077.
Values may be sent and summed in bfloat16 or wider, within the bound.
A program may use at most 192 MiB of HBM per device.

v0:
```python
import functools

import jax
import jax.numpy as jnp
from jax import lax
from jax.experimental import pallas as pl
from jax.experimental.pallas import tpu as pltpu
from jax.sharding import PartitionSpec as P

BF, F32 = jnp.bfloat16, jnp.float32
MESH = pl.DeviceIdType.MESH
JT = 16
CLASSES = ((0, 1), (2, 3), (4,))
ND = 5


def where_am_i():
    aa, ba = lax.axis_index("aa"), lax.axis_index("ba")
    core, z = lax.rem(aa, 2), lax.rem(lax.div(aa, 2), 4)
    x = 2 * lax.div(aa, 8) + lax.rem(ba, 2)
    y = lax.div(ba, 2)
    return aa, ba, x, y, z, core


def place(x, y, z, core):
    aa = 8 * lax.div(x, 2) + 2 * z + core
    ba = 2 * y + lax.rem(x, 2)
    return aa, ba


def masks(step):
    one = step ^ (step >> 2)
    mx, my, mz, mc = (one ^ (step >> 4)) & 3, one & 3, step & 3, (step ^ (step >> 6)) & 1
    return ((mx >> 1) << 3) | (mz << 1) | mc, (my << 1) | (mx & 1)


def total_wait(ref, sem):
    pltpu.make_async_copy(ref, ref, sem).wait()


def kernel(
    field, m1_hbm, m2_hbm, out,
    fbuf, tbuf, obuf, sbuf, rbuf, m1, m1t, m2, m2buf, m2t, cacc, cc, acc, fr, tr, pmat,
    fsem, wsem, send, recv, m2send, m2recv, m2sem, csend, crecv, gsend, grecv, osend, frecv, trecv, wsend, wrecv, *parts,
):
    gs, r1, s1, r2, s2, r3 = (parts[3 * n : 3 * n + 3] for n in range(6))
    aa, ba, x, y, z, core = where_am_i()
    tiles = fbuf.shape[0]
    sibling = {"aa": aa + 1 - 2 * core, "ba": ba}
    place_in_k = 8 * core + 4 * lax.div(x, 2) + z

    def load(tile, part):
        rows = pl.ds(256 * part, 256)
        return pltpu.make_async_copy(
            field.at[rows, pl.ds(JT * tile, JT), :], fbuf.at[tile, rows], fsem.at[tile, part]
        )

    load_m1 = pltpu.make_async_copy(m1_hbm, m1, wsem.at[0])
    load_m2 = pltpu.make_async_copy(m2_hbm, m2, wsem.at[1])
    load_m1.start()
    for part in range(4):
        load(0, part).start()
    load_m2.start()

    barrier = pltpu.get_barrier_semaphore()

    def greet(aa_mask, ba_mask):
        pl.semaphore_signal(
            barrier, inc=1, device_id={"aa": aa ^ aa_mask, "ba": ba ^ ba_mask}, device_id_type=MESH
        )

    for ba_mask in range(1, 8):
        greet(0, ba_mask)

    @pl.loop(1, 16)
    def _(aa_mask):
        for ba_mask in range(8):
            greet(aa_mask, ba_mask)

    for tile in range(1, tiles):
        for part in range(4):
            load(tile, part).start()

    row = lax.broadcasted_iota(jnp.int32, (256, 256), 0)
    col = lax.broadcasted_iota(jnp.int32, (256, 256), 1)
    swap = ((row & 15) * 16 + (row >> 4)) == col
    pmat[...] = jnp.where(swap, 1.0, 0.0).astype(BF)
    load_m1.wait()
    m1t[...] = m1[...].T

    def send_rows(tile, first, count, sem):
        rows = pl.ds(pl.multiple_of(JT * place_in_k, JT), JT)

        def block(to_aa, to_ba):
            mine = sbuf.at[tile, pl.ds(2 * (8 * to_aa + to_ba) + first, count)]
            return mine, rbuf.at[tile, pl.ds(first, count), ba, rows, :]

        @pl.loop(1, 128)
        def _(step):
            aa_mask, ba_mask = masks(step)
            to_aa, to_ba = aa ^ aa_mask, ba ^ ba_mask
            mine, there = block(to_aa, to_ba)
            pltpu.make_async_remote_copy(
                mine, there, send, sem, device_id={"aa": to_aa, "ba": to_ba}, device_id_type=MESH
            ).start()

        mine, there = block(aa, ba)
        pltpu.make_async_copy(mine, there, sem).start()

    @pl.loop(0, tiles)
    def _(tile):
        @pl.loop(0, 4)
        def _(part):
            load(tile, part).wait()

            @pl.loop(0, 8, unroll=4)
            def _(group):
                at = pl.multiple_of(256 * part + 32 * group, 32)
                left = fbuf[tile, pl.ds(at, 16)].reshape(256, 128)
                right = fbuf[tile, pl.ds(at + 16, 16)].reshape(256, 128)
                both = jnp.concatenate([left, right], axis=1)
                turned = jnp.dot(pmat[...], both, preferred_element_type=F32).astype(BF)
                tbuf[:, pl.ds(at, 16), :] = turned[:, :128].reshape(16, 16, 128)
                tbuf[:, pl.ds(pl.multiple_of(at + 16, 16), 16), :] = turned[:, 128:].reshape(16, 16, 128)

        @pl.loop(0, JT // 2)
        def _(pair):
            both = jnp.concatenate([tbuf[2 * pair], tbuf[2 * pair + 1]], axis=1)
            got = jnp.dot(m1t[...], both, preferred_element_type=F32).astype(BF)
            obuf[2 * pair] = got[:, :128]
            obuf[2 * pair + 1] = got[:, 128:]

        @pl.loop(0, 8, unroll=2)
        def _(group):
            at = pl.multiple_of(32 * group, 32)
            left = obuf[:, pl.ds(at, 16), :].reshape(256, 128)
            right = obuf[:, pl.ds(pl.multiple_of(at + 16, 16), 16), :].reshape(256, 128)
            both = jnp.concatenate([left, right], axis=1)
            turned = jnp.dot(pmat[...], both, preferred_element_type=F32).astype(BF)
            sbuf[tile, pl.ds(at, 16)] = turned[:, :128].reshape(16, 16, 128)
            sbuf[tile, pl.ds(at + 16, 16)] = turned[:, 128:].reshape(16, 16, 128)

        @pl.when(tile == 0)
        def _():
            pl.semaphore_wait(barrier, 127)

        @pl.when(tile < 3)
        def _():
            send_rows(tile, 0, 2, recv.at[tile])

        @pl.when(tile == 3)
        def _():
            for half in range(2):
                send_rows(tile, half, 1, recv.at[3 + half])

        @pl.when(tile == 1)
        def _():
            load_m2.wait()
            mine = m2buf.at[:, place_in_k]
            for mask in range(1, 8):
                to_aa, to_ba = place(x ^ (2 * (mask // 4)), y, z ^ (mask % 4), core)
                pltpu.make_async_remote_copy(
                    m2, mine, m2send, m2recv, device_id={"aa": to_aa, "ba": to_ba}, device_id_type=MESH
                ).start()
            pltpu.make_async_copy(m2, mine, m2recv).start()

    half_of_m2 = m2buf.at[:, pl.ds(8 * core, 8)]
    total_wait(half_of_m2, m2recv)
    pass_m2 = pltpu.make_async_remote_copy(
        half_of_m2, half_of_m2, m2sem.at[0], m2sem.at[1], device_id=sibling, device_id_type=MESH
    )
    pass_m2.start()
    pass_m2.wait()
    for tile in range(4):
        m2t[tile] = m2buf[tile].reshape(256, 256).T

    def share(half):
        return pltpu.make_async_remote_copy(
            cc.at[:, pl.ds(256 * half, 256), :], cc.at[:, pl.ds(512 + 256 * half, 256), :],
            csend.at[half], crecv.at[half], device_id=sibling, device_id_type=MESH,
        )

    for tile in range(4):
        if tile < 3:
            total_wait(rbuf.at[tile], recv.at[tile])
        for half in range(2):
            if tile == 3:
                total_wait(rbuf.at[tile, half], recv.at[3 + half])

            @pl.loop(0, 4, unroll=2)
            def _(pair):
                both = jnp.concatenate([rbuf[tile, half, 2 * pair], rbuf[tile, half, 2 * pair + 1]], axis=1)
                got = jnp.dot(m2t[tile], both, preferred_element_type=F32)
                if tile > 0:
                    got += cacc[half, pair]
                if tile < 3:
                    cacc[half, pair] = got
                else:
                    cc[2 * pair, pl.ds(256 * half, 256), :] = got[:, :128].astype(BF)
                    cc[2 * pair + 1, pl.ds(256 * half, 256), :] = got[:, 128:].astype(BF)

            if tile == 3:
                share(half).start()

    where = (x, y, z)

    def term(block_row, first):
        rows = pl.ds(first, 512)
        right = jnp.concatenate([cc[lax.rem(block_row + d, 8), rows, :] for d in range(ND)], axis=1)
        return lax.dot_general(
            cc[block_row, rows, :], right, (((0,), (0,)), ((), ())), preferred_element_type=F32
        )

    def pieces(got, low_y, low_x):
        for octet in range(16):
            owner = (2 * (octet >> 3) + low_x, 2 * (octet & 1) + low_y, (octet >> 1) & 3)
            for k, columns in enumerate(CLASSES):
                index = tuple(owner[(k + stage) % 3] for stage in range(3))
                for n, d in enumerate(columns):
                    yield gs[k], index + (n,), got[8 * octet : 8 * octet + 8, 128 * d : 128 * d + 128]

    for low_y in range(2):
        for low_x in range(2):
            for ref, index, value in pieces(term(4 * core + 2 * low_y + low_x, 0), low_y, low_x):
                ref[index] = value
    for half in range(2):
        share(half).wait()
    for low_y in range(2):
        for low_x in range(2):
            for ref, index, value in pieces(term(4 * core + 2 * low_y + low_x, 512), low_y, low_x):
                ref[index] += value

    def scatter(k, stage):
        axis = (k + stage) % 3
        for mask in range(1, 4):
            there = [x, y, z]
            there[axis] = there[axis] ^ mask
            to_aa, to_ba = place(*there, core)
            pltpu.make_async_remote_copy(
                sums[stage][k].at[where[axis] ^ mask], got_from[stage][k].at[mask - 1], gsend, grecv.at[k, stage],
                device_id={"aa": to_aa, "ba": to_ba}, device_id_type=MESH,
            ).start()

    def gathered(k, stage):
        total_wait(got_from[stage][k], grecv.at[k, stage])
        got = got_from[stage][k]
        return sums[stage][k][where[(k + stage) % 3]] + got[0] + got[1] + got[2]

    sums = (gs, s1, s2)
    got_from = (r1, r2, r3)
    for k in range(3):
        scatter(k, 0)
    for stage in range(2):
        for k in range(3):
            sums[stage + 1][k][...] = gathered(k, stage)
            scatter(k, stage + 1)
    for k, columns in enumerate(CLASSES):
        acc[pl.ds(columns[0], len(columns))] = gathered(k, 2) * (1.0 / 65536.0)

    mine = 4 * core + 2 * lax.rem(y, 2) + lax.rem(x, 2)
    own = pl.ds(pl.multiple_of(8 * (8 * lax.div(x, 2) + 2 * z + lax.div(y, 2)), 8), 8)
    inside = jnp.logical_and(mine == ba, lax.div(x, 2) == core)

    taker = lax.div(x, 2)

    @pl.loop(0, 8)
    def _(step):
        to_aa = (aa ^ (2 * step) ^ core) | taker
        self = jnp.logical_and(inside, step == 0)

        @pl.when(self)
        def _():
            pltpu.make_async_copy(acc, fr.at[:, own, :], frecv).start()

        @pl.when(jnp.logical_not(self))
        def _():
            pltpu.make_async_remote_copy(
                acc, fr.at[:, own, :], osend, frecv,
                device_id={"aa": to_aa, "ba": mine}, device_id_type=MESH,
            ).start()

        for d in range(1, 4):
            pltpu.make_async_remote_copy(
                acc.at[d], tr.at[d - 1, own, :], osend, trecv,
                device_id={"aa": to_aa, "ba": lax.rem(mine + d, 8)}, device_id_type=MESH,
            ).start()

    half = pl.ds(pl.multiple_of(64 * core, 64), 64)
    swaps = []
    for n, (ref, sem) in enumerate(((fr, frecv), (tr, trecv))):
        total_wait(ref.at[:, half, :], sem)
        swaps.append(pltpu.make_async_remote_copy(
            ref.at[:, half, :], ref.at[:, half, :], wsend.at[n], wrecv.at[n],
            device_id=sibling, device_id_type=MESH,
        ))
        swaps[n].start()

    swaps[0].wait()
    for d in range(ND):
        out[:, pl.ds(pl.multiple_of(128 * lax.rem(ba + d, 8), 128), 128)] = fr[d]
    swaps[1].wait()
    for d in range(1, 4):
        out[:, pl.ds(pl.multiple_of(128 * lax.rem(ba + 8 - d, 8), 128), 128)] = tr[d - 1].T

    total_wait(sbuf.at[:, pl.ds(0, 254)], send)
    total_wait(m2buf.at[:, pl.ds(0, 7)], m2send)
    for stage in range(3):
        for k in range(3):
            total_wait(got_from[stage][k], gsend)
    total_wait(fr.at[:, pl.ds(0, 56), :], osend)

    @pl.when(jnp.logical_not(inside))
    def _():
        total_wait(fr.at[:, pl.ds(0, 8), :], osend)

    total_wait(tr.at[:, pl.ds(0, 64), :], osend)


def shards(field, mode_one, mode_two):
    dma = pltpu.SemaphoreType.DMA
    hbm = pl.BlockSpec(memory_space=pltpu.HBM)
    return pl.pallas_call(
        kernel,
        out_shape=jax.ShapeDtypeStruct((128, 1024), F32),
        in_specs=[hbm, hbm, hbm],
        out_specs=pl.BlockSpec(memory_space=pltpu.VMEM),
        scratch_shapes=[
            pltpu.VMEM((4, 1024, JT, 128), BF),
            pltpu.VMEM((JT, 1024, 128), BF),
            pltpu.VMEM((JT, 256, 128), BF),
            pltpu.VMEM((4, 256, JT, 128), BF),
            pltpu.VMEM((4, 2, 8, 256, 128), BF),
            pltpu.VMEM((1024, 256), BF),
            pltpu.VMEM((256, 1024), BF),
            pltpu.VMEM((4, JT, 256), BF),
            pltpu.VMEM((4, 16, JT, 256), BF),
            pltpu.VMEM((4, 256, 256), BF),
            pltpu.VMEM((2, 4, 256, 256), F32),
            pltpu.VMEM((8, 1024, 128), BF),
            pltpu.VMEM((ND, 8, 128), F32),
            pltpu.VMEM((ND, 128, 128), F32),
            pltpu.VMEM((3, 128, 128), F32),
            pltpu.VMEM((256, 256), BF),
            dma((4, 4)), dma((2,)),
            dma, dma((5,)), dma, dma, dma((2,)),
            dma((2,)), dma((2,)),
            dma, dma((3, 3)), dma, dma, dma, dma((2,)), dma((2,)),
            *[
                pltpu.VMEM(shape + (len(columns), 8, 128), F32)
                for shape in ((4, 4, 4), (3, 4, 4), (4, 4), (3, 4), (4,), (3,))
                for columns in CLASSES
            ],
        ],
        compiler_params=pltpu.CompilerParams(
            collective_id=0, has_side_effects=True, vmem_limit_bytes=53 * 1024 * 1024
        ),
        cost_estimate=pl.CostEstimate(flops=13_000_000_000, bytes_accessed=18_000_000, transcendentals=0),
    )(field, mode_one, mode_two.reshape(4, JT, 256))


def solution(mesh):
    in_specs = (P(None, "aa", "ba"), P(), P("aa", None))
    return jax.shard_map(shards, mesh=mesh, in_specs=in_specs, out_specs=P("ba", None), check_vma=False)
```

profile of v0, /device:TPU:1, one launch (start us, length us, event | category | flops | bytes accessed | tf_op | source)
XLA Modules:
  0.0 94.7 jit_solution(15185412330526006333)
XLA Ops:
  0.0 0.0 copy-start
  0.0 0.8 copy-done
  0.8 93.2 %shard_map.37 = f32[128,1024]{1,0:T(8,128)S(1)} custom-call(bf16[1024,64,128]{2,1,0:T(8,128)(2,1)} %field.1, bf16[1024,256]{1,0:T(8,128)(2,1)} %m1_hbm.1, bf16[4,16,256]{2,1,0:T(8,128)(2,1)S(1)} %bitcast.1), custom_call_target="tpu_custom_call" | custom-call | flops 12999999488 | bytes 18000000 | tf_op jit(solution)/shard_map/pallas_call | solution.py:322
  93.9 0.8 copy.5
Async XLA Ops:
  0.0 0.8 copy-start
where the time goes:
time: 94.9 us; the launch traced here: 94.7 us
  Pallas kernels  93.2 us (98%)
  local copies, waits for them, and re-layouts  1.55 us (2%)
    pallas_call x1, Pallas kernels, shards(): pl.pallas_call(kernel, out_shape=jax.ShapeDtypeStruct((128, 1024), F32),...  93.2 us

commit v1 on v0

--- a/solution.py
+++ b/solution.py
@@ -41,7 +41,7 @@
 def kernel(
     field, m1_hbm, m2_hbm, out,
     fbuf, tbuf, obuf, sbuf, rbuf, m1, m1t, m2, m2buf, m2t, cacc, cc, acc, fr, tr, pmat,
-    fsem, wsem, send, recv, m2send, m2recv, m2sem, csend, crecv, gsend, grecv, osend, frecv, trecv, wsend, wrecv, *parts,
+    fsem, wsem, send, recv, m2send, m2recv, m2sem, m2ysend, m2yrecv, csend, crecv, gsend, grecv, osend, frecv, trecv, wsend, wrecv, *parts,
 ):
     gs, r1, s1, r2, s2, r3 = (parts[3 * n : 3 * n + 3] for n in range(6))
     aa, ba, x, y, z, core = where_am_i()
@@ -55,27 +55,27 @@
             field.at[rows, pl.ds(JT * tile, JT), :], fbuf.at[tile, rows], fsem.at[tile, part]
         )
 
+    barrier = pltpu.get_barrier_semaphore()
+
+    def greet(aa_mask, ba_mask):
+        pl.semaphore_signal(
+            barrier, inc=1, device_id={"aa": aa ^ aa_mask, "ba": ba ^ ba_mask}, device_id_type=MESH
+        )
+
+    for ba_mask in range(1, 8):
+        greet(0, ba_mask)
+
+    @pl.loop(1, 16)
+    def _(aa_mask):
+        for ba_mask in range(8):
+            greet(aa_mask, ba_mask)
+
     load_m1 = pltpu.make_async_copy(m1_hbm, m1, wsem.at[0])
     load_m2 = pltpu.make_async_copy(m2_hbm, m2, wsem.at[1])
     load_m1.start()
     for part in range(4):
         load(0, part).start()
     load_m2.start()
-
-    barrier = pltpu.get_barrier_semaphore()
-
-    def greet(aa_mask, ba_mask):
-        pl.semaphore_signal(
-            barrier, inc=1, device_id={"aa": aa ^ aa_mask, "ba": ba ^ ba_mask}, device_id_type=MESH
-        )
-
-    for ba_mask in range(1, 8):
-        greet(0, ba_mask)
-
-    @pl.loop(1, 16)
-    def _(aa_mask):
-        for ba_mask in range(8):
-            greet(aa_mask, ba_mask)
 
     for tile in range(1, tiles):
         for part in range(4):
@@ -106,6 +106,16 @@
 
         mine, there = block(aa, ba)
         pltpu.make_async_copy(mine, there, sem).start()
+
+    parity = lax.rem(y, 2)
+
+    def trade_m2(n):
+        gathered = m2buf.at[parity + 2 * n, pl.ds(8 * core, 8)]
+        to_aa, to_ba = place(x, y ^ (1 + 2 * n), z, core)
+        return pltpu.make_async_remote_copy(
+            gathered, gathered, m2ysend.at[n], m2yrecv.at[n],
+            device_id={"aa": to_aa, "ba": to_ba}, device_id_type=MESH,
+        )
 
     @pl.loop(0, tiles)
     def _(tile):
@@ -153,19 +163,30 @@
             for half in range(2):
                 send_rows(tile, half, 1, recv.at[3 + half])
 
-        @pl.when(tile == 1)
+        @pl.when(tile == 0)
         def _():
             load_m2.wait()
-            mine = m2buf.at[:, place_in_k]
             for mask in range(1, 8):
                 to_aa, to_ba = place(x ^ (2 * (mask // 4)), y, z ^ (mask % 4), core)
-                pltpu.make_async_remote_copy(
-                    m2, mine, m2send, m2recv, device_id={"aa": to_aa, "ba": to_ba}, device_id_type=MESH
+                for n in range(2):
+                    pltpu.make_async_remote_copy(
+                        m2.at[parity + 2 * n], m2buf.at[parity + 2 * n, place_in_k], m2send, m2recv,
+                        device_id={"aa": to_aa, "ba": to_ba}, device_id_type=MESH,
+                    ).start()
+            for n in range(2):
+                pltpu.make_async_copy(
+                    m2.at[parity + 2 * n], m2buf.at[parity + 2 * n, place_in_k], m2recv
                 ).start()
-            pltpu.make_async_copy(m2, mine, m2recv).start()
-
+
+        @pl.when(tile == 2)
+        def _():
+            total_wait(m2buf.at[pl.ds(0, 2), pl.ds(0, 8)], m2recv)
+            for n in range(2):
+                trade_m2(n).start()
+
+    for n in range(2):
+        trade_m2(n).wait()
     half_of_m2 = m2buf.at[:, pl.ds(8 * core, 8)]
-    total_wait(half_of_m2, m2recv)
     pass_m2 = pltpu.make_async_remote_copy(
         half_of_m2, half_of_m2, m2sem.at[0], m2sem.at[1], device_id=sibling, device_id_type=MESH
     )
@@ -303,7 +324,7 @@
         out[:, pl.ds(pl.multiple_of(128 * lax.rem(ba + 8 - d, 8), 128), 128)] = tr[d - 1].T
 
     total_wait(sbuf.at[:, pl.ds(0, 254)], send)
-    total_wait(m2buf.at[:, pl.ds(0, 7)], m2send)
+    total_wait(m2buf.at[pl.ds(0, 2), pl.ds(0, 7)], m2send)
     for stage in range(3):
         for k in range(3):
             total_wait(got_from[stage][k], gsend)
@@ -342,7 +363,7 @@
             pltpu.VMEM((3, 128, 128), F32),
             pltpu.VMEM((256, 256), BF),
             dma((4, 4)), dma((2,)),
-            dma, dma((5,)), dma, dma, dma((2,)),
+            dma, dma((5,)), dma, dma, dma((2,)), dma((2,)), dma((2,)),
             dma((2,)), dma((2,)),
             dma, dma((3, 3)), dma, dma, dma, dma((2,)), dma((2,)),
             *[

time: 94.9 us -> 94.6 us (level)
  no operation moved by 1% of the time
where the time goes in v1:
time: 94.6 us; the launch traced here: 94.4 us
  Pallas kernels  92.8 us (98%)
  local copies, waits for them, and re-layouts  1.55 us (2%)
    pallas_call x1, Pallas kernels, shards(): pl.pallas_call(kernel, out_shape=jax.ShapeDtypeStruct((128, 1024), F32),...  92.8 us

profile of v1, /device:TPU:1, one launch (start us, length us, event | category | flops | bytes accessed | tf_op | source)
XLA Modules:
  0.0 94.4 jit_solution(4607857482883279391)
XLA Ops:
  0.0 0.0 copy-start
  0.0 0.8 copy-done
  0.8 92.8 %shard_map.37 = f32[128,1024]{1,0:T(8,128)S(1)} custom-call(bf16[1024,64,128]{2,1,0:T(8,128)(2,1)} %field.1, bf16[1024,256]{1,0:T(8,128)(2,1)} %m1_hbm.1, bf16[4,16,256]{2,1,0:T(8,128)(2,1)S(1)} %bitcast.1), custom_call_target="tpu_custom_call" | custom-call | flops 12999999488 | bytes 18000000 | tf_op jit(solution)/shard_map/pallas_call | solution.py:343
  93.6 0.8 copy.5
Async XLA Ops:
  0.0 0.8 copy-start
